TPU v7x, 32 devices: a whole 2x2x4 slice. The times are simulated.
32 devices in a mesh: blk: 16 (over z, y, x), day: 2 (over core).
Axes of the slice: x: 2, y: 2, z: 4, core: 2. Of those that a mesh axis runs over, the one named last changes fastest.
Arguments:
- input_field: float32 [2, 6, 128, 4096], P(None, 'day', 'blk'), may hold values from -6 to 6
- active_mask: int32 [128], P('blk'), may hold values from 0 to 1, as said below
- neighbours: int32 [128, 8], P('blk'), may hold values from -1 to 127, as said below
- time_taps: float32 [4], replicated, may hold values from 0.1 to 0.5
- space_taps: float32 [2, 5], replicated, may hold values from 0.1 to 0.5
- coregion_factor: float32 [2, 2], replicated, may hold values from -2.5 to 2.5
Outputs:
- covariance_product: float32 [2, 6, 128, 4096], P(None, 'day', 'blk')
Inputs may be any that keep to these rules, and one draw needn't show every extreme that they name: `active_mask`: device i along blk holds in its 8 slots, in a drawn order, the map positions i * 8 to i * 8 + 7 of a map of 4 rows of 32 positions numbered row by row; every position of the first two map rows is active, others are active at random. Entries name the global slot (device index along blk times 8 plus local slot) of the active map block beside the block in that direction, -1 where there is none or it is inactive; all entries of an inactive slot are -1. East and west neighbours are held by the same device or one place away along blk; north and south ones by the device 4 places away; the four diagonal ones by the device 4 places away or one place nearer or farther than that, and all these cases occur.
All inputs are finite; a program needn't handle non-finite values.
Results may differ from a plain program's by a relative error of at most 0.0003.
Values sent between devices are 32-bit elements; how exact they have to be, the bound alone decides.
No kernel may reach another device: no remote copies, remote signals or barrier semaphores. Data moves between devices by JAX's collectives and lax.ppermute only.
A program may use at most 64 MiB of HBM per device.

v0:
```python
import functools

import jax
import jax.numpy as jnp
from jax import lax
from jax.experimental import pallas as pl
from jax.experimental.pallas import tpu as pltpu
from jax.sharding import PartitionSpec as P

SIDE = 64
SPACE_HALF = 4
TIME_HALF = 3
REACH = 4
LANES = 128
EAST, WEST, NORTH, SOUTH, NORTH_EAST, NORTH_WEST, SOUTH_EAST, SOUTH_WEST = range(8)
PAIR_ROWS = SPACE_HALF * SIDE // LANES
GROUPS = SIDE // SPACE_HALF
BESIDE, UPPER, LOWER, EAST_FLAG, SOUTH_FLAG, PLANS = 0, 3, 8, 13, 14, 15
PARAMS = pltpu.CompilerParams(vmem_limit_bytes=12 * 1024 * 1024)
SMEM = pl.BlockSpec(memory_space=pltpu.SMEM)
WHOLE = pl.BlockSpec(memory_space=pltpu.VMEM)
IN_HBM = pl.BlockSpec(memory_space=pltpu.HBM)
DMA = pltpu.SemaphoreType.DMA


def array(*shape):
    return jax.ShapeDtypeStruct(shape, jnp.float32)


def iotas(slots):
    lane = lax.broadcasted_iota(jnp.int32, (slots, LANES), 1)
    sublane = lax.broadcasted_iota(jnp.int32, (slots, LANES), 0)
    return lane, sublane


def live_vector(mask_ref, sublane):
    live = jnp.zeros(sublane.shape, jnp.float32)
    for slot in range(sublane.shape[0]):
        live = jnp.where(sublane == slot, mask_ref[slot].astype(jnp.float32), live)
    return live


def entry(neighbours, direction, shape):
    return jnp.broadcast_to(neighbours[:, direction : direction + 1], shape)


def pick(source, index):
    return jnp.take_along_axis(source, index, axis=0)


def roll(x, shift):
    return pltpu.roll(x, shift % LANES if isinstance(shift, int) else shift, 1)


def wrapped(shift):
    return jnp.bitwise_and(shift, LANES - 1)


def device_of(target, slots):
    return lax.shift_right_arithmetic(target, jnp.int32(slots.bit_length() - 1))


def on_device(target, device, slots):
    return (target >= 0) & (device_of(target, slots) == device)


def taps_of(taps_ref):
    return [taps_ref[lag] for lag in range(TIME_HALF + 1)]


def order_of(pair, day, days):
    return [day * (days - 1 - 2 * s) + s if pair else s for s in range(days)]


def coupling_of(factor_ref):
    return [
        [
            factor_ref[a, 0] * factor_ref[b, 0] + factor_ref[a, 1] * factor_ref[b, 1]
            for b in range(2)
        ]
        for a in range(2)
    ]


def same_days(taps, values):
    totals = []
    for t in range(len(values)):
        total = taps[0] * values[t]
        for s in range(len(values)):
            if s != t:
                total = total + taps[abs(s - t)] * values[s]
        totals.append(total)
    return totals


def add_later(taps, totals, values):
    for t in range(len(totals)):
        for s in range(t + 1):
            totals[t] = totals[t] + taps[len(totals) + s - t] * values[s]


def add_earlier(taps, totals, values):
    for t in range(len(totals)):
        for s in range(t, len(totals)):
            totals[t] = totals[t] + taps[len(totals) + t - s] * values[s]


def east_first(place_ref):
    return jnp.bitwise_and(place_ref[0], 1) == 0


def south_first(place_ref):
    return jnp.bitwise_and(place_ref[0], REACH) == 0


def end_slot(nb_ref, me, east):
    slots = nb_ref.shape[0]
    step, directions = (
        (1, (EAST, NORTH_EAST, SOUTH_EAST)) if east else (-1, (WEST, NORTH_WEST, SOUTH_WEST))
    )
    found = jnp.int32(0)
    for slot in range(slots):
        for direction, shift in zip(directions, (0, -REACH, REACH)):
            target = nb_ref[slot, direction]
            hit = (target >= 0) & (device_of(target, slots) == me + step + shift)
            found = jnp.where(hit, slot, found)
    return found


def edge_plan(place_ref, nb_ref):
    me = place_ref[0]
    east, west = end_slot(nb_ref, me, True), end_slot(nb_ref, me, False)
    first = east_first(place_ref)
    return [(first, jnp.where(first, east, west)), (~first, jnp.where(first, west, east))]


def strip_starts(place_ref, tiles):
    last = tiles - PAIR_ROWS
    first = south_first(place_ref)
    return [jnp.where(first, last, 0), jnp.where(first, 0, last)]


def own_kernel(place_ref, mask_ref, taps_ref, _, nb_ref, x_ref, own_ref, *edge_refs):
    comps, days, tiles, slots, _ = x_ref.shape
    taps = taps_of(taps_ref)
    for edge_ref, (_, slot) in zip(edge_refs, edge_plan(place_ref, nb_ref)):
        live = mask_ref[slot].astype(jnp.float32)
        for comp in range(comps):
            for t in range(days):
                edge_ref[comp * days + t] = live * x_ref[comp, t, :, slot, :]
    def body(tile, _):
        for comp in range(comps):
            values = [x_ref[comp, t, tile] for t in range(days)]
            for t, total in enumerate(same_days(taps, values)):
                own_ref[comp * days + t, tile] = total
        return 0

    lax.fori_loop(0, tiles, body, 0, unroll=4)


def all_days(pair, place_ref, taps_ref, factor_ref, raw_ref, other_refs, read_other):
    comps, days = other_refs[0].shape[:2]
    taps = taps_of(taps_ref)
    coupling = coupling_of(factor_ref)
    order = order_of(pair, place_ref[1], days)
    filtered = []
    for comp in range(comps):
        totals = same_days(taps, [raw_ref[comp * days + order[s]] for s in range(days)])
        later = [read_other(other_refs[-1], comp, order[s]) for s in range(days)]
        add_later(taps, totals, later)
        if not pair:
            earlier = [read_other(other_refs[0], comp, s) for s in range(days)]
            add_earlier(taps, totals, earlier)
        filtered.append(totals)
    for a in range(comps):
        for t in range(days):
            value = coupling[a][0] * filtered[0][t] + coupling[a][1] * filtered[1][t]
            yield a * days + order[t], value


def edge_kernel(pair, place_ref, mask_ref, taps_ref, factor_ref, nb_ref, *refs):
    raw_refs, other_refs, packed_refs = refs[:2], refs[2:-2], refs[-2:]
    tiles = other_refs[0].shape[2]
    column = jnp.bitwise_and(lax.broadcasted_iota(jnp.int32, (tiles, LANES), 1), SIDE - 1)
    group = lax.shift_right_logical(column, jnp.int32(SPACE_HALF.bit_length() - 1))
    for raw_ref, packed_ref, (to_east, slot) in zip(
        raw_refs, packed_refs, edge_plan(place_ref, nb_ref)
    ):
        live = mask_ref[slot].astype(jnp.float32)
        packed = jnp.zeros((tiles, LANES), jnp.float32)
        for at, value in all_days(
            pair, place_ref, taps_ref, factor_ref, raw_ref, other_refs,
            lambda ref, c, s: live * ref[c, s, :, slot, :],
        ):
            shift = wrapped(jnp.where(to_east, LANES - SPACE_HALF * at, SPACE_HALF * at))
            spot = jnp.where(to_east, GROUPS - 1 - at, at)
            packed = jnp.where(group == spot, roll(value, shift), packed)
        packed_ref[...] = packed


def two_parts(x):
    coarse = x.astype(jnp.bfloat16)
    return coarse, (x - coarse.astype(jnp.float32)).astype(jnp.bfloat16)


def build_plans(place_ref, mask_ref, space_ref, nb_ref, level_ref, plan_ref):
    shape = level_ref.shape[1:]
    slots = shape[0]
    nb = nb_ref[...]
    me = place_ref[0]
    for lag in range(SPACE_HALF + 1):
        level_ref[lag] = jnp.full(shape, space_ref[1, lag], jnp.float32)
    level_ref[SPACE_HALF + 1] = live_vector(mask_ref, iotas(slots)[1])

    def put_sides(at, west, east, device):
        index, near, remote = sides_of(nb, west, east, device, shape)
        plan_ref[at] = index
        plan_ref[at + 1] = near.astype(jnp.int32)
        plan_ref[at + 2] = remote.astype(jnp.int32)

    put_sides(BESIDE, WEST, EAST, me)
    put_sides(UPPER, NORTH_WEST, NORTH_EAST, me - REACH)
    put_sides(LOWER, SOUTH_WEST, SOUTH_EAST, me + REACH)
    for at, direction in ((UPPER, NORTH), (LOWER, SOUTH)):
        target = entry(nb, direction, shape)
        plan_ref[at + 3] = jnp.bitwise_and(target, slots - 1)
        plan_ref[at + 4] = (target >= 0).astype(jnp.int32)
    plan_ref[EAST_FLAG] = jnp.full(shape, jnp.where(east_first(place_ref), 1, 0), jnp.int32)
    plan_ref[SOUTH_FLAG] = jnp.full(shape, jnp.where(south_first(place_ref), 1, 0), jnp.int32)


def plan_at(plan_ref, at):
    return plan_ref[at], plan_ref[at + 1] != 0, plan_ref[at + 2] != 0


def flag_of(plan_ref, at, rows):
    return jnp.broadcast_to(plan_ref[at, :1], (rows, LANES)) != 0


def build_bands(taps_ref, bands_ref):
    shape = (2 * LANES, LANES)
    source = lax.broadcasted_iota(jnp.int32, shape, 0)
    target = lax.broadcasted_iota(jnp.int32, shape, 1)
    same = jnp.bitwise_and(source // SIDE, 1) == target // SIDE
    source_column = jnp.bitwise_and(source, SIDE - 1)
    outside = jnp.where(source_column >= SIDE // 2, source_column - SIDE, source_column + SIDE)
    position = jnp.where(source < LANES, source_column, outside)
    distance = jnp.abs(position - jnp.bitwise_and(target, SIDE - 1))
    bands = jnp.zeros(shape, jnp.float32)
    for lag in range(SPACE_HALF + 1):
        bands = jnp.where(same & (distance == lag), taps_ref[0, lag], bands)
    coarse, fine = two_parts(bands)
    bands_ref[: 2 * LANES, :LANES] = coarse
    bands_ref[: 2 * LANES, LANES:] = fine
    bands_ref[2 * LANES :, :LANES] = coarse
    bands_ref[2 * LANES :, LANES:] = jnp.zeros_like(fine)


def mix_kernel(
    pair, place_ref, mask_ref, taps_ref, factor_ref, space_ref, nb_ref, own_ref, *rest
):
    *other_refs, mixed_ref, first_ref, second_ref, bands_ref, level_ref, plan_ref = rest
    build_bands(space_ref, bands_ref)
    build_plans(place_ref, mask_ref, space_ref, nb_ref, level_ref, plan_ref)
    _, tiles, slots, _ = mixed_ref.shape
    comps, days = other_refs[0].shape[:2]
    _, sublane = iotas(slots)
    live = live_vector(mask_ref, sublane)
    taps = taps_of(taps_ref)
    weights = [[live * value for value in row] for row in coupling_of(factor_ref)]
    order = order_of(pair, place_ref[1], days)

    def body(tile, _):
        filtered = []
        for comp in range(comps):
            totals = [own_ref[comp * days + order[t], tile] for t in range(days)]
            add_later(taps, totals, [other_refs[-1][comp, order[s], tile] for s in range(days)])
            if not pair:
                add_earlier(taps, totals, [other_refs[0][comp, s, tile] for s in range(days)])
            filtered.append(totals)
        for a in range(comps):
            for t in range(days):
                mixed_ref[a * days + order[t], tile] = (
                    weights[a][0] * filtered[0][t] + weights[a][1] * filtered[1][t]
                )
        return 0

    lax.fori_loop(0, tiles, body, 0, unroll=4)
    for sent_ref, start in zip((first_ref, second_ref), strip_starts(place_ref, tiles)):
        for item in range(comps * days):
            sent_ref[item] = mixed_ref[item, pl.ds(start, PAIR_ROWS)]


def west_east(plan_ref, first, second):
    flag = flag_of(plan_ref, EAST_FLAG, first.shape[0])
    return jnp.where(flag, second, first), jnp.where(flag, first, second)


def unpacked(item, west, east):
    column = jnp.bitwise_and(lax.broadcasted_iota(jnp.int32, west.shape, 1), SIDE - 1)
    return jnp.where(
        column >= SIDE // 2,
        roll(west, wrapped(SPACE_HALF * item)),
        roll(east, wrapped(LANES - SPACE_HALF * item)),
    )


def corner_kernel(plan_ref, second_ref, first_ref, *refs):
    one_ref, two_ref = refs[-2:]
    slots = one_ref.shape[2]
    south = flag_of(plan_ref, SOUTH_FLAG, slots)
    for k, side in enumerate(west_east(plan_ref, first_ref[...], second_ref[...])):
        top, bottom = side[:slots], side[-slots:]
        one_ref[0, k] = jnp.where(south, bottom, top)
        two_ref[0, k] = jnp.where(south, top, bottom)


def across(bands, tiles):
    slots = tiles[0][0].shape[0]
    centre_parts = two_parts(jnp.concatenate([centre for centre, _ in tiles], axis=0))
    halo_parts = two_parts(jnp.concatenate([halo for _, halo in tiles], axis=0))
    product = jnp.dot(
        jnp.concatenate([part for both in zip(centre_parts, halo_parts) for part in both], axis=1),
        bands,
        preferred_element_type=jnp.float32,
    )
    product = product[:, :LANES] + product[:, LANES:]
    return [product[slots * p : slots * (p + 1)] for p in range(len(tiles))]


def sides_of(nb, west, east, device, shape):
    slots = shape[0]
    column = jnp.bitwise_and(lax.broadcasted_iota(jnp.int32, shape, 1), SIDE - 1)
    target = jnp.where(column >= SIDE // 2, entry(nb, west, shape), entry(nb, east, shape))
    near = on_device(target, device, slots)
    return jnp.bitwise_and(target, slots - 1), near, (target >= 0) & ~near


def halo_of(source, far, plan):
    index, near, remote = plan
    halo = jnp.where(near, pick(source, index), 0.0)
    return jnp.where(remote, jnp.broadcast_to(far, halo.shape), halo)


def odd_rows(before, after):
    low = lax.broadcasted_iota(jnp.int32, before.shape, 1) < SIDE
    return roll(jnp.where(low, after, before), SIDE)


def inner_kernel(
    level_ref, plan_ref, bands_ref, mixed_ref, second_ref, first_ref,
    out_hbm, outer_ref, out_ref, far_ref, stored,
):
    count, tiles, slots, _ = mixed_ref.shape
    lane, sublane = iotas(slots)
    live = level_ref[SPACE_HALF + 1]
    taps = [level_ref[lag] for lag in range(SPACE_HALF + 1)]
    plan = plan_at(plan_ref, BESIDE)
    west, east = west_east(plan_ref, first_ref[...], second_ref[...])
    together = far_ref.shape[0]

    def store(step):
        part = pl.ds(step * together, together)
        return pltpu.make_async_copy(out_ref.at[part], out_hbm.at[part], stored.at[step])

    def body(step, _):
        fetched = []
        for k in range(together):
            item = step * together + k
            far_ref[k] = unpacked(item, west, east)
            for tile in range(tiles):
                centre = mixed_ref[item, tile]
                fetched.append((centre, halo_of(centre, far_ref[k, tile : tile + 1], plan)))
        lines = across(bands_ref[...], fetched)
        zero = jnp.zeros(lane.shape, jnp.float32)
        for k in range(together):
            item = step * together + k
            rows = [zero] * PAIR_ROWS + lines[k * tiles : (k + 1) * tiles] + [zero] * PAIR_ROWS
            odd = [odd_rows(rows[p], rows[p + 1]) for p in range(len(rows) - 1)]
            for p in range(tiles):
                total = taps[0] * rows[p + 2]
                total = total + taps[1] * (odd[p + 1] + odd[p + 2])
                total = total + taps[2] * (rows[p + 1] + rows[p + 3])
                total = total + taps[3] * (odd[p] + odd[p + 3])
                total = total + taps[4] * (rows[p] + rows[p + 4])
                total = live * total
                out_ref[item, p] = total
                if p < PAIR_ROWS:
                    outer_ref[item, p] = total
                elif p >= tiles - PAIR_ROWS:
                    outer_ref[item, p - tiles + 2 * PAIR_ROWS] = total
        store(step).start()
        return 0

    lax.fori_loop(0, count // together, body, 0)
    for step in range(count // together):
        store(step).wait()


def outer_kernel(
    level_ref, plan_ref, bands_ref, outer_ref, first_ref, second_ref,
    _, out_hbm, out_ref, stored,
):
    count, _, slots, _ = outer_ref.shape
    tiles = out_hbm.shape[1]
    lane, sublane = iotas(slots)
    live = level_ref[SPACE_HALF + 1]
    taps = [level_ref[lag] for lag in range(SPACE_HALF + 1)]
    south = plan_ref[SOUTH_FLAG] != 0
    fetched = []
    for north in (True, False):
        use_first = ~south if north else south

        def read(index, part, use_first=use_first):
            return jnp.where(use_first, first_ref[index, part], second_ref[index, part])

        at = UPPER if north else LOWER
        plan = plan_at(plan_ref, at)
        index, present = plan_ref[at + 3], plan_ref[at + 4] != 0
        corner = [read(count, 0), read(count, 1)]
        for item in range(count):
            far = unpacked(jnp.int32(item), *corner)
            for part in range(PAIR_ROWS):
                source = read(item, part)
                centre = jnp.where(present, pick(source, index), 0.0)
                row = slots - PAIR_ROWS + part if north else part
                fetched.append((centre, halo_of(source, far[row : row + 1], plan)))
    rows = across(bands_ref[...], fetched)
    zero = jnp.zeros(lane.shape, jnp.float32)
    copies = []
    for side in range(2):
        for item in range(count):
            at = (side * count + item) * PAIR_ROWS
            one, two = rows[at : at + PAIR_ROWS]
            close, far = (one, two) if side else (two, one)
            edge = odd_rows(zero, one) if side else odd_rows(two, zero)
            near = taps[1] * edge + taps[2] * close + taps[3] * odd_rows(one, two)
            near = near + taps[4] * far
            off = taps[3] * edge + taps[4] * close
            for part, value in enumerate((off, near) if side else (near, off)):
                out_ref[side, item, part] = (
                    outer_ref[item, side * PAIR_ROWS + part] + live * value
                )
        place = pl.ds(side * (tiles - PAIR_ROWS), PAIR_ROWS)
        copy = pltpu.make_async_copy(out_ref.at[side], out_hbm.at[:, place], stored.at[side])
        copy.start()
        copies.append(copy)
    for copy in copies:
        copy.wait()


def swap_both(first, second, index, length):
    blk, day = lax.axis_size("blk"), lax.axis_size("day")
    results = []
    for x, shift in ((first, 0), (second, 1)):
        partner = {}
        for at in range(shift, length + shift, 2):
            low, high = at % length, (at + 1) % length
            partner[low], partner[high] = high, low
        pairs = []
        for i in range(blk):
            at, step = index(i)
            across_chip = day == 2 and abs(partner[at] - at) > 1
            other = i if across_chip else i + (partner[at] - at) * step
            for core in range(day):
                pairs.append((i * day + core, other * day + (1 - core if across_chip else core)))
        results.append(lax.ppermute(x, ("blk", "day"), pairs))
    return results


def shards(input_field, active_mask, neighbours, time_taps, space_taps, coregion_factor):
    comps, days, slots, cells = input_field.shape
    count = comps * days
    tiles = cells // LANES
    blk = lax.axis_size("blk")
    day = lax.axis_size("day")
    pair = day == 2
    sides = 2
    place = jnp.stack([lax.axis_index("blk"), lax.axis_index("day")]).astype(jnp.int32)

    def in_tiles(x):
        return x.reshape(comps, days, slots, tiles, LANES).transpose(0, 1, 3, 2, 4)

    if pair:
        others = [lax.ppermute(input_field, "day", [(0, 1), (1, 0)])]
    else:
        up = [(i, i + 1) for i in range(day - 1)]
        others = [
            lax.ppermute(input_field, "day", up),
            lax.ppermute(input_field, "day", [(b, a) for a, b in up]),
        ]
    others = [in_tiles(x) for x in others]
    field = array(count, tiles, slots, LANES)

    own, *raw = pl.pallas_call(
        own_kernel,
        out_shape=(field,) + (array(count, tiles, LANES),) * 2,
        in_specs=[SMEM] * 5 + [WHOLE],
        out_specs=(WHOLE,) * 3,
        compiler_params=PARAMS,
        name="own_days",
    )(place, active_mask, time_taps, coregion_factor, neighbours, in_tiles(input_field))

    sent_count = count + 1
    sent_shape = array(sent_count, PAIR_ROWS, slots, LANES)
    packed = pl.pallas_call(
        functools.partial(edge_kernel, pair),
        out_shape=(array(tiles, LANES),) * 2,
        in_specs=[SMEM] * 5 + [WHOLE] * (2 + len(others)),
        out_specs=(WHOLE,) * 2,
        compiler_params=PARAMS,
        name="edges",
    )(place, active_mask, time_taps, coregion_factor, neighbours, *raw, *others)
    first, second = swap_both(*packed, lambda i: (i % REACH, 1), REACH)

    mixed, *sent, bands, level, plan = pl.pallas_call(
        functools.partial(mix_kernel, pair),
        out_shape=(
            field,
            sent_shape,
            sent_shape,
            jax.ShapeDtypeStruct((4 * LANES, 2 * LANES), jnp.bfloat16),
            array(SPACE_HALF + 2, slots, LANES),
            jax.ShapeDtypeStruct((PLANS, slots, LANES), jnp.int32),
        ),
        in_specs=[SMEM] * 5 + [WHOLE] * (2 + len(others)),
        out_specs=(WHOLE,) * 6,
        compiler_params=PARAMS,
        cost_estimate=pl.CostEstimate(
            flops=20 * field.size, bytes_accessed=12 * field.size, transcendentals=0
        ),
        name="mix",
    )(place, active_mask, time_taps, coregion_factor, space_taps, neighbours, own, *others)

    sent = pl.pallas_call(
        corner_kernel,
        grid=(1,),
        out_shape=(sent_shape,) * sides,
        in_specs=[WHOLE] * 3 + [pl.BlockSpec(memory_space=pl.ANY)] * (sides + 1),
        out_specs=(
            pl.BlockSpec((1, PAIR_ROWS, slots, LANES), lambda i: (sent_count - 1, 0, 0, 0)),
        )
        * sides,
        input_output_aliases={4 + side: side for side in range(sides)},
        compiler_params=PARAMS,
        name="corners",
    )(plan, second, first, mixed, *sent)

    one, two = swap_both(*sent, lambda i: (i // REACH, REACH), blk // REACH)

    together = 2
    inner, outer = pl.pallas_call(
        inner_kernel,
        out_shape=(field, array(count, 2 * PAIR_ROWS, slots, LANES)),
        in_specs=[WHOLE] * 6,
        out_specs=(IN_HBM, WHOLE),
        scratch_shapes=[
            pltpu.VMEM(field.shape, jnp.float32),
            pltpu.VMEM((together, tiles, LANES), jnp.float32),
            DMA((count // together,)),
        ],
        compiler_params=PARAMS,
        cost_estimate=pl.CostEstimate(
            flops=4 * field.size * LANES, bytes_accessed=8 * field.size, transcendentals=0
        ),
        name="inner_rows",
    )(level, plan, bands, mixed, second, first)

    result = pl.pallas_call(
        outer_kernel,
        out_shape=field,
        in_specs=[WHOLE] * 6 + [IN_HBM],
        out_specs=IN_HBM,
        scratch_shapes=[
            pltpu.VMEM((2, count, PAIR_ROWS, slots, LANES), jnp.float32),
            DMA((2,)),
        ],
        input_output_aliases={6: 0},
        compiler_params=PARAMS,
        name="outer_rows",
    )(level, plan, bands, outer, one, two, inner)
    result = result.reshape(comps, days, tiles, slots, LANES).transpose(0, 1, 3, 2, 4)
    return result.reshape(input_field.shape)


def solution(mesh):
    in_specs = (P(None, "day", "blk", None), P("blk"), P("blk", None), P(), P(), P())
    out_specs = P(None, "day", "blk", None)
    return jax.shard_map(shards, mesh=mesh, in_specs=in_specs, out_specs=out_specs, check_vma=False)
```

profile of v0, /device:TPU:18, one launch (start us, length us, event | category | flops | bytes accessed | tf_op | source)
XLA Modules:
  0.0 16.2 jit_solution(1281266166400990133)
XLA Ops:
  0.0 0.0 collective-permute-start
  0.0 0.0 copy-start.1
  0.0 0.0 copy-start.4
  0.0 0.1 pad_add_fusion.place_ref
  0.1 0.6 %copy-done.1 = s32[8,8]{1,0:T(8,128)S(1)} copy-done((s32[8,8]{1,0:T(8,128)S(1)}, s32[8,8]{1,0:T(8,128)}, u32[]{:S(2)}) %copy-start.1) | copy-done | bytes 280
  0.7 0.0 copy-done.4
  0.7 0.1 copy-done.2
  0.8 0.0 copy-done.3
  0.8 1.1 %copy-done = f32[2,3,8,4096]{3,2,1,0:T(8,128)S(1)} copy-done((f32[2,3,8,4096]{3,2,1,0:T(8,128)S(1)}, f32[2,3,8,4096]{3,2,1,0:T(8,128)}, u32[]{:S(2)}) %copy-start) | copy-done | bytes 786456
  1.9 1.0 %own_days.1 = (f32[6,32,8,128]{3,2,1,0:T(8,128)S(1)}, f32[6,32,128]{2,1,0:T(8,128)S(1)}, f32[6,32,128]{2,1,0:T(8,128)S(1)}) custom-call(s32[2]{0:T(128)S(1)} %pad_add_fusion.place_ref, s32[8]{0:T(128)S(1)} %copy-done.3, f32[4]{0:T(128)S(1)} %copy-done.4, f32[2,2]{1,0:T(2,128)S(1)} %copy-done.2, s32[8,8]{1,0:T(8,128)S(1)} %copy-done.1, ...), custom_call_target="tpu_custom_call" | custom-call | tf_op jit(solution)/shard_map/own_days/pallas_call | solution.py:495
  2.9 0.0 collective-permute-done
  2.9 1.2 %edges.1 = (f32[32,128]{1,0:T(8,128)S(1)}, f32[32,128]{1,0:T(8,128)S(1)}) custom-call(s32[2]{0:T(128)S(1)} %pad_add_fusion.place_ref, s32[8]{0:T(128)S(1)} %copy-done.3, f32[4]{0:T(128)S(1)} %copy-done.4, f32[2,2]{1,0:T(2,128)S(1)} %copy-done.2, s32[8,8]{1,0:T(8,128)S(1)} %copy-done.1, f32[6,32,128]{2,1,0:T(8,128)S(1)} %get-tuple-element.25.refs_0_, ...), custom_call_target="tpu_custom_call" | custom-call | tf_op jit(solution)/shard_map/edges/pallas_call | solution.py:506
  4.1 1.6 %collective-permute-start.1 = (f32[32,128]{1,0:T(8,128)S(1)}, f32[32,128]{1,0:T(8,128)S(1)}, u32[]{:S(2)}, u32[]{:S(2)}) collective-permute-start(f32[32,128]{1,0:T(8,128)S(1)} %get-tuple-element.27), channel_id=1, source_target_pairs={{0,1},{1,0},{2,4},{3,5},{4,2},{5,3},{6,7},{7,6},{8,9},{9,8},{10,12... | collective-permute-start | bytes 49160 | tf_op jit(solution)/shard_map/ppermute | solution.py:467
  5.7 0.0 collective-permute-start.2
  5.7 0.7 %copy-done.5 = f32[2,5]{1,0:T(2,128)S(1)} copy-done((f32[2,5]{1,0:T(2,128)S(1)}, f32[2,5]{1,0:T(2,128)}, u32[]{:S(2)}) %copy-start.5) | copy-done | bytes 64
  6.4 1.0 %mix.1 = (f32[6,32,8,128]{3,2,1,0:T(8,128)S(1)}, f32[7,2,8,128]{3,2,1,0:T(8,128)S(1)}, f32[7,2,8,128]{3,2,1,0:T(8,128)S(1)}, bf16[512,256]{1,0:T(8,128)(2,1)S(1)...) custom-call(s32[2]{0:T(128)S(1)} %pad_add_fusion.place_ref, s32[8]{0:T(128)S(1)} %copy-done.3, f32[4]{0:T(128)S(1)} %copy-done.4, ...), custom_call_target="tpu_custom_call" | custom-call | flops 3932160 | bytes 2359296 | tf_op jit(solution)/shard_map/mix/pallas_call | solution.py:516
  7.4 1.4 %collective-permute-done.1.second_ref = f32[32,128]{1,0:T(8,128)S(1)} collective-permute-done((f32[32,128]{1,0:T(8,128)S(1)}, f32[32,128]{1,0:T(8,128)S(1)}, u32[]{:S(2)}, u32[]{:S(2)}) %collective-permute-start.1) | collective-permute-done | bytes 16416 | tf_op jit(solution)/shard_map/ppermute | solution.py:467
  8.8 0.6 %collective-permute-done.2.first_ref = f32[32,128]{1,0:T(8,128)S(1)} collective-permute-done((f32[32,128]{1,0:T(8,128)S(1)}, f32[32,128]{1,0:T(8,128)S(1)}, u32[]{:S(2)}, u32[]{:S(2)}) %collective-permute-start.2) | collective-permute-done | bytes 16416 | tf_op jit(solution)/shard_map/ppermute | solution.py:467
  9.4 1.6 %collective-permute-start.3 = (f32[7,2,8,128]{3,2,1,0:T(8,128)S(1)}, f32[7,2,8,128]{3,2,1,0:T(8,128)S(1)}, u32[]{:S(2)}, u32[]{:S(2)}) collective-permute-start(f32[7,2,8,128]{3,2,1,0:T(8,128)S(1)} %get-tuple-element.32), channel_id=1, source_target_pairs={{0,8},{1,9},{2,10},{3,11},{4,12},{5,13},{6,14},{7,15},{8,0},{9,1},... | collective-permute-start | bytes 172040 | tf_op jit(solution)/shard_map/ppermute | solution.py:467
  11.0 0.0 collective-permute-start.4
  11.0 2.1 %inner_rows.1 = (f32[6,32,8,128]{3,2,1,0:T(8,128)}, f32[6,4,8,128]{3,2,1,0:T(8,128)S(1)}) custom-call(f32[6,8,128]{2,1,0:T(8,128)S(1)} %get-tuple-element.21.level_ref, s32[15,8,128]{2,1,0:T(8,128)S(1)} %get-tuple-element.22.plan_ref, bf16[512,256]{1,0:T(8,128)(2,1)S(1)} %get-tuple-element.23.bands_ref, ...), custom_call_target="tpu_custom_call" | custom-call | flops 100663296 | bytes 1572864 | tf_op jit(solution)/shard_map/inner_rows/pallas_call | solution.py:552
  13.1 0.5 %collective-permute-done.3.first_ref = f32[7,2,8,128]{3,2,1,0:T(8,128)S(1)} collective-permute-done((f32[7,2,8,128]{3,2,1,0:T(8,128)S(1)}, f32[7,2,8,128]{3,2,1,0:T(8,128)S(1)}, u32[]{:S(2)}, u32[]{:S(2)}) %collective-permute-start.3) | collective-permute-done | bytes 57376 | tf_op jit(solution)/shard_map/ppermute | solution.py:467
  13.6 1.6 %collective-permute-done.4.second_ref = f32[7,2,8,128]{3,2,1,0:T(8,128)S(1)} collective-permute-done((f32[7,2,8,128]{3,2,1,0:T(8,128)S(1)}, f32[7,2,8,128]{3,2,1,0:T(8,128)S(1)}, u32[]{:S(2)}, u32[]{:S(2)}) %collective-permute-start.4) | collective-permute-done | bytes 57376 | tf_op jit(solution)/shard_map/ppermute | solution.py:467
  15.2 1.0 %outer_rows.1 = f32[6,32,8,128]{3,2,1,0:T(8,128)} custom-call(f32[6,8,128]{2,1,0:T(8,128)S(1)} %get-tuple-element.21.level_ref, s32[15,8,128]{2,1,0:T(8,128)S(1)} %get-tuple-element.22.plan_ref, bf16[512,256]{1,0:T(8,128)(2,1)S(1)} %get-tuple-element.23.bands_ref, f32[6,4,8,128]{3,2,1,0:T(8,128)S(1)} %get-tuple-element.29.outer_ref, ...), custom_call_target="tpu_custom_call", output_to_operand_aliasing={{}: (6, {})} | custom-call | tf_op jit(solution)/shard_map/outer_rows/pallas_call | solution.py:569
  (5 shorter events, 0.0 us)
Async XLA Ops:
  0.0 2.9 %collective-permute-start = (f32[2,3,8,4096]{3,2,1,0:T(8,128)}, f32[2,3,8,4096]{3,2,1,0:T(8,128)S(1)}, u32[]{:S(2)}, u32[]{:S(2)}) collective-permute-start(f32[2,3,8,4096]{3,2,1,0:T(8,128)} %param.6), channel_id=1, source_target_pairs={{0,1},{1,0},{2,3},{3,2},{4,5},{5,4},{6,7},{7,6},{8,9},{9,8},{10,11... | collective-permute-start | bytes 2359304 | tf_op jit(solution)/shard_map/ppermute | solution.py:485
  0.0 0.7 %copy-start.1 = (s32[8,8]{1,0:T(8,128)S(1)}, s32[8,8]{1,0:T(8,128)}, u32[]{:S(2)}) copy-start(s32[8,8]{1,0:T(8,128)} %nb_ref.5) | copy-start | bytes 772
  0.0 0.7 %copy-start.4 = (f32[4]{0:T(128)S(1)}, f32[4]{0:T(128)}, u32[]{:S(2)}) copy-start(f32[4]{0:T(128)} %taps_ref.5) | copy-start | bytes 52
  0.1 0.7 %copy-start.2 = (f32[2,2]{1,0:T(2,128)S(1)}, f32[2,2]{1,0:T(2,128)}, u32[]{:S(2)}) copy-start(f32[2,2]{1,0:T(2,128)} %factor_ref.3) | copy-start | bytes 52
  0.1 0.7 %copy-start.3 = (s32[8]{0:T(128)S(1)}, s32[8]{0:T(128)}, u32[]{:S(2)}) copy-start(s32[8]{0:T(128)} %mask_ref.5) | copy-start | bytes 100
  0.8 1.1 %copy-start = (f32[2,3,8,4096]{3,2,1,0:T(8,128)S(1)}, f32[2,3,8,4096]{3,2,1,0:T(8,128)}, u32[]{:S(2)}) copy-start(f32[2,3,8,4096]{3,2,1,0:T(8,128)} %param.6) | copy-start | bytes 2359300
  4.1 4.7 %collective-permute-start.1 = (f32[32,128]{1,0:T(8,128)S(1)}, f32[32,128]{1,0:T(8,128)S(1)}, u32[]{:S(2)}, u32[]{:S(2)}) collective-permute-start(f32[32,128]{1,0:T(8,128)S(1)} %get-tuple-element.27), channel_id=1, source_target_pairs={{0,1},{1,0},{2,4},{3,5},{4,2},{5,3},{6,7},{7,6},{8,9},{9,8},{10,12... | collective-permute-start | bytes 49160 | tf_op jit(solution)/shard_map/ppermute | solution.py:467
  5.7 0.7 %copy-start.5 = (f32[2,5]{1,0:T(2,128)S(1)}, f32[2,5]{1,0:T(2,128)}, u32[]{:S(2)}) copy-start(f32[2,5]{1,0:T(2,128)} %space_ref.1) | copy-start | bytes 124
  5.7 3.7 %collective-permute-start.2 = (f32[32,128]{1,0:T(8,128)S(1)}, f32[32,128]{1,0:T(8,128)S(1)}, u32[]{:S(2)}, u32[]{:S(2)}) collective-permute-start(f32[32,128]{1,0:T(8,128)S(1)} %get-tuple-element.28), channel_id=1, source_target_pairs={{0,2},{1,3},{2,0},{3,1},{4,6},{5,7},{6,4},{7,5},{8,10},{9,11},{10,... | collective-permute-start | bytes 49160 | tf_op jit(solution)/shard_map/ppermute | solution.py:467
  9.4 4.2 %collective-permute-start.3 = (f32[7,2,8,128]{3,2,1,0:T(8,128)S(1)}, f32[7,2,8,128]{3,2,1,0:T(8,128)S(1)}, u32[]{:S(2)}, u32[]{:S(2)}) collective-permute-start(f32[7,2,8,128]{3,2,1,0:T(8,128)S(1)} %get-tuple-element.32), channel_id=1, source_target_pairs={{0,8},{1,9},{2,10},{3,11},{4,12},{5,13},{6,14},{7,15},{8,0},{9,1},... | collective-permute-start | bytes 172040 | tf_op jit(solution)/shard_map/ppermute | solution.py:467
  11.0 4.2 %collective-permute-start.4 = (f32[7,2,8,128]{3,2,1,0:T(8,128)S(1)}, f32[7,2,8,128]{3,2,1,0:T(8,128)S(1)}, u32[]{:S(2)}, u32[]{:S(2)}) collective-permute-start(f32[7,2,8,128]{3,2,1,0:T(8,128)S(1)} %get-tuple-element.33), channel_id=1, source_target_pairs={{0,1},{1,0},{2,3},{3,2},{4,5},{5,4},{6,7},{7,6},{8,16},{9,17},{10,... | collective-permute-start | bytes 172040 | tf_op jit(solution)/shard_map/ppermute | solution.py:467
where the time goes:
time: 16.4 us; the launch traced here: 16.2 us
  Pallas kernels  6.27 us (38%)
  waiting for transfers between devices  4.14 us (25%)
  starting transfers between devices  3.14 us (19%)
  local copies, waits for them, and re-layouts  2.49 us (15%)
    ppermute x4, waiting for transfers between devices, swap_both(): results.append(lax.ppermute(x, ('blk', 'day'), pairs))  4.13 us
    ppermute x4, starting transfers between devices, swap_both(): results.append(lax.ppermute(x, ('blk', 'day'), pairs))  3.14 us
    unnamed x12, local copies, waits for them, and re-layouts  2.49 us
    pallas_call x1, Pallas kernels, shards(): pl.pallas_call(inner_kernel, out_shape=(field, array(count, 2 * PAIR_ROWS...  2.07 us
    pallas_call x1, Pallas kernels, shards(): pl.pallas_call(functools.partial(edge_kernel, pair), out_shape=(array(til...  1.2 us
    pallas_call x1, Pallas kernels, shards(): pl.pallas_call(functools.partial(mix_kernel, pair), out_shape=(field, sen...  1.02 us
    pallas_call x1, Pallas kernels, shards(): pl.pallas_call(own_kernel, out_shape=(field,) + (array(count, tiles, LANE...  1.01 us
    pallas_call x1, Pallas kernels, shards(): pl.pallas_call(outer_kernel, out_shape=field, in_specs=[WHOLE] * 6 + [IN_...  0.97 us
  transfers between devices with their start and end apart: 5, of which 4 were waited for; matrix products, arithmetic and copies ran while one was open for 0% of the time, Pallas kernels for 25%

commit v1 on v0

--- a/solution.py
+++ b/solution.py
@@ -16,6 +16,7 @@
 PAIR_ROWS = SPACE_HALF * SIDE // LANES
 GROUPS = SIDE // SPACE_HALF
 BESIDE, UPPER, LOWER, EAST_FLAG, SOUTH_FLAG, PLANS = 0, 3, 8, 13, 14, 15
+PICK, COUPLING, TAPS, LATER, EARLIER, EAST_LEVEL, VALUES = 0, 16, 20, 24, 33, 42, 43
 PARAMS = pltpu.CompilerParams(vmem_limit_bytes=12 * 1024 * 1024)
 SMEM = pl.BlockSpec(memory_space=pltpu.SMEM)
 WHOLE = pl.BlockSpec(memory_space=pltpu.VMEM)
@@ -140,10 +141,43 @@
     return [jnp.where(first, last, 0), jnp.where(first, 0, last)]
 
 
-def own_kernel(place_ref, mask_ref, taps_ref, _, nb_ref, x_ref, own_ref, *edge_refs):
+def write_values(pair, place_ref, mask_ref, taps, factor_ref, ends, value_ref):
+    shape = value_ref.shape[1:]
+    slots = shape[0]
+    days = len(taps) - 1
+
+    def put(at, value):
+        value_ref[at] = jnp.full(shape, value, jnp.float32)
+
+    for k, (_, slot) in enumerate(ends):
+        live = mask_ref[slot].astype(jnp.float32)
+        for s in range(slots):
+            put(PICK + k * slots + s, jnp.where(slot == s, live, 0.0))
+    for a, row in enumerate(coupling_of(factor_ref)):
+        for b, value in enumerate(row):
+            put(COUPLING + 2 * a + b, value)
+    for lag, value in enumerate(taps):
+        put(TAPS + lag, value)
+    for t in range(days):
+        for s in range(days):
+            later = taps[days + s - t] if s <= t else 0.0
+            earlier = taps[days + t - s] if s >= t else 0.0
+            if pair:
+                later = jnp.where(place_ref[1] == 0, later, earlier)
+            put(LATER + t * days + s, later)
+            put(EARLIER + t * days + s, earlier)
+    put(EAST_LEVEL, jnp.where(east_first(place_ref), 1.0, 0.0))
+
+
+def own_kernel(
+    pair, place_ref, mask_ref, taps_ref, factor_ref, nb_ref, x_ref, own_ref, *refs
+):
+    *edge_refs, value_ref = refs
     comps, days, tiles, slots, _ = x_ref.shape
     taps = taps_of(taps_ref)
-    for edge_ref, (_, slot) in zip(edge_refs, edge_plan(place_ref, nb_ref)):
+    ends = edge_plan(place_ref, nb_ref)
+    write_values(pair, place_ref, mask_ref, taps, factor_ref, ends, value_ref)
+    for edge_ref, (_, slot) in zip(edge_refs, ends):
         live = mask_ref[slot].astype(jnp.float32)
         for comp in range(comps):
             for t in range(days):
@@ -158,43 +192,46 @@
     lax.fori_loop(0, tiles, body, 0, unroll=4)
 
 
-def all_days(pair, place_ref, taps_ref, factor_ref, raw_ref, other_refs, read_other):
-    comps, days = other_refs[0].shape[:2]
-    taps = taps_of(taps_ref)
-    coupling = coupling_of(factor_ref)
-    order = order_of(pair, place_ref[1], days)
-    filtered = []
-    for comp in range(comps):
-        totals = same_days(taps, [raw_ref[comp * days + order[s]] for s in range(days)])
-        later = [read_other(other_refs[-1], comp, order[s]) for s in range(days)]
-        add_later(taps, totals, later)
-        if not pair:
-            earlier = [read_other(other_refs[0], comp, s) for s in range(days)]
-            add_earlier(taps, totals, earlier)
-        filtered.append(totals)
-    for a in range(comps):
-        for t in range(days):
-            value = coupling[a][0] * filtered[0][t] + coupling[a][1] * filtered[1][t]
-            yield a * days + order[t], value
-
-
-def edge_kernel(pair, place_ref, mask_ref, taps_ref, factor_ref, nb_ref, *refs):
+def edge_kernel(pair, value_ref, *refs):
     raw_refs, other_refs, packed_refs = refs[:2], refs[2:-2], refs[-2:]
-    tiles = other_refs[0].shape[2]
+    comps, days, tiles, slots, _ = other_refs[0].shape
     column = jnp.bitwise_and(lax.broadcasted_iota(jnp.int32, (tiles, LANES), 1), SIDE - 1)
     group = lax.shift_right_logical(column, jnp.int32(SPACE_HALF.bit_length() - 1))
-    for raw_ref, packed_ref, (to_east, slot) in zip(
-        raw_refs, packed_refs, edge_plan(place_ref, nb_ref)
-    ):
-        live = mask_ref[slot].astype(jnp.float32)
+
+    def level(at):
+        return jnp.concatenate([value_ref[at]] * (tiles // slots), axis=0)
+
+    taps = [level(TAPS + lag) for lag in range(TIME_HALF + 1)]
+    sources = [(other_refs[-1], LATER)] + ([] if pair else [(other_refs[0], EARLIER)])
+    filtered = [[], []]
+    for comp in range(comps):
+        totals = [
+            same_days(taps, [raw_ref[comp * days + s] for s in range(days)]) for raw_ref in raw_refs
+        ]
+        for source, base in sources:
+            for s in range(days):
+                edges = [None, None]
+                for slot in range(slots):
+                    value = source[comp, s, :, slot, :]
+                    for k in range(2):
+                        term = level(PICK + k * slots + slot) * value
+                        edges[k] = term if edges[k] is None else edges[k] + term
+                for t in range(days):
+                    factor = level(base + t * days + s)
+                    for k in range(2):
+                        totals[k][t] = totals[k][t] + factor * edges[k]
+        for k in range(2):
+            filtered[k].append(totals[k])
+    for k, packed_ref in enumerate(packed_refs):
+        to_east = (level(EAST_LEVEL) > 0.5) if k == 0 else (level(EAST_LEVEL) < 0.5)
         packed = jnp.zeros((tiles, LANES), jnp.float32)
-        for at, value in all_days(
-            pair, place_ref, taps_ref, factor_ref, raw_ref, other_refs,
-            lambda ref, c, s: live * ref[c, s, :, slot, :],
-        ):
-            shift = wrapped(jnp.where(to_east, LANES - SPACE_HALF * at, SPACE_HALF * at))
-            spot = jnp.where(to_east, GROUPS - 1 - at, at)
-            packed = jnp.where(group == spot, roll(value, shift), packed)
+        for a in range(comps):
+            for t in range(days):
+                at = a * days + t
+                value = level(COUPLING + 2 * a) * filtered[k][0][t]
+                value = value + level(COUPLING + 2 * a + 1) * filtered[k][1][t]
+                spot = jnp.where(to_east, GROUPS - 1 - at, -at % GROUPS)
+                packed = jnp.where(group == spot, roll(value, -SPACE_HALF * at), packed)
         packed_ref[...] = packed
 
 
@@ -297,12 +334,10 @@
 
 
 def unpacked(item, west, east):
-    column = jnp.bitwise_and(lax.broadcasted_iota(jnp.int32, west.shape, 1), SIDE - 1)
-    return jnp.where(
-        column >= SIDE // 2,
-        roll(west, wrapped(SPACE_HALF * item)),
-        roll(east, wrapped(LANES - SPACE_HALF * item)),
-    )
+    lane = lax.broadcasted_iota(jnp.int32, west.shape, 1)
+    shift = SPACE_HALF * item
+    from_west = jnp.bitwise_and(lane + shift, SIDE // 2) != 0
+    return roll(jnp.where(from_west, west, east), shift)
 
 
 def corner_kernel(plan_ref, second_ref, first_ref, *refs):
@@ -419,7 +454,7 @@
         index, present = plan_ref[at + 3], plan_ref[at + 4] != 0
         corner = [read(count, 0), read(count, 1)]
         for item in range(count):
-            far = unpacked(jnp.int32(item), *corner)
+            far = unpacked(item, *corner)
             for part in range(PAIR_ROWS):
                 source = read(item, part)
                 centre = jnp.where(present, pick(source, index), 0.0)
@@ -492,11 +527,13 @@
     others = [in_tiles(x) for x in others]
     field = array(count, tiles, slots, LANES)
 
-    own, *raw = pl.pallas_call(
-        own_kernel,
-        out_shape=(field,) + (array(count, tiles, LANES),) * 2,
+    own, *raw, values = pl.pallas_call(
+        functools.partial(own_kernel, pair),
+        out_shape=(field,)
+        + (array(count, tiles, LANES),) * 2
+        + (array(VALUES, slots, LANES),),
         in_specs=[SMEM] * 5 + [WHOLE],
-        out_specs=(WHOLE,) * 3,
+        out_specs=(WHOLE,) * 4,
         compiler_params=PARAMS,
         name="own_days",
     )(place, active_mask, time_taps, coregion_factor, neighbours, in_tiles(input_field))
@@ -506,11 +543,11 @@
     packed = pl.pallas_call(
         functools.partial(edge_kernel, pair),
         out_shape=(array(tiles, LANES),) * 2,
-        in_specs=[SMEM] * 5 + [WHOLE] * (2 + len(others)),
+        in_specs=[WHOLE] * (3 + len(others)),
         out_specs=(WHOLE,) * 2,
         compiler_params=PARAMS,
         name="edges",
-    )(place, active_mask, time_taps, coregion_factor, neighbours, *raw, *others)
+    )(values, *raw, *others)
     first, second = swap_both(*packed, lambda i: (i % REACH, 1), REACH)
 
     mixed, *sent, bands, level, plan = pl.pallas_call(

time: 16.4 us -> 15.9 us (0.970)
  Pallas kernels: 6.27 us -> 5.74 us
    pallas_call x1, Pallas kernels: 1.2 us -> 0.69 us  [shards(): pl.pallas_call(functools.partial(edge_kernel, pair), out_shape=(array(til...]
  transfers between devices with their start and end apart: 5 -> 5, of which waited for: 4 -> 4; matrix products, arithmetic and copies ran while one was open for 0% -> 0% of each run, Pallas kernels for 25% -> 26%
where the time goes in v1:
time: 15.9 us; the launch traced here: 15.7 us
  Pallas kernels  5.74 us (36%)
  waiting for transfers between devices  4.16 us (26%)
  starting transfers between devices  3.14 us (20%)
  local copies, waits for them, and re-layouts  2.49 us (16%)
    ppermute x4, waiting for transfers between devices, swap_both(): results.append(lax.ppermute(x, ('blk', 'day'), pairs))  4.15 us
    ppermute x4, starting transfers between devices, swap_both(): results.append(lax.ppermute(x, ('blk', 'day'), pairs))  3.14 us
    unnamed x12, local copies, waits for them, and re-layouts  2.49 us
    pallas_call x1, Pallas kernels, shards(): pl.pallas_call(inner_kernel, out_shape=(field, array(count, 2 * PAIR_ROWS...  2.05 us
    pallas_call x1, Pallas kernels, shards(): pl.pallas_call(functools.partial(mix_kernel, pair), out_shape=(field, sen...  1.02 us
    pallas_call x1, Pallas kernels, shards(): pl.pallas_call(functools.partial(own_kernel, pair), out_shape=(field,) +...  1.01 us
    pallas_call x1, Pallas kernels, shards(): pl.pallas_call(outer_kernel, out_shape=field, in_specs=[WHOLE] * 6 + [IN_...  0.97 us
    pallas_call x1, Pallas kernels, shards(): pl.pallas_call(functools.partial(edge_kernel, pair), out_shape=(array(til...  0.69 us
  transfers between devices with their start and end apart: 5, of which 4 were waited for; matrix products, arithmetic and copies ran while one was open for 0% of the time, Pallas kernels for 26%

profile of v1, /device:TPU:18, one launch (start us, length us, event | category | flops | bytes accessed | tf_op | source)
XLA Modules:
  0.0 15.7 jit_solution(10669538628219380185)
XLA Ops:
  0.0 0.0 collective-permute-start
  0.0 0.0 copy-start.1
  0.0 0.0 copy-start.4
  0.0 0.1 pad_add_fusion.place_ref
  0.1 0.6 %copy-done.1 = s32[8,8]{1,0:T(8,128)S(1)} copy-done((s32[8,8]{1,0:T(8,128)S(1)}, s32[8,8]{1,0:T(8,128)}, u32[]{:S(2)}) %copy-start.1) | copy-done | bytes 280
  0.7 0.0 copy-done.4
  0.7 0.1 copy-done.2
  0.8 0.0 copy-done.3
  0.8 1.1 %copy-done = f32[2,3,8,4096]{3,2,1,0:T(8,128)S(1)} copy-done((f32[2,3,8,4096]{3,2,1,0:T(8,128)S(1)}, f32[2,3,8,4096]{3,2,1,0:T(8,128)}, u32[]{:S(2)}) %copy-start) | copy-done | bytes 786456
  1.9 1.0 %own_days.1 = (f32[6,32,8,128]{3,2,1,0:T(8,128)S(1)}, f32[6,32,128]{2,1,0:T(8,128)S(1)}, f32[6,32,128]{2,1,0:T(8,128)S(1)}, f32[43,8,128]{2,1,0:T(8,128)S(1)}) custom-call(s32[2]{0:T(128)S(1)} %pad_add_fusion.place_ref, s32[8]{0:T(128)S(1)} %copy-done.3, f32[4]{0:T(128)S(1)} %copy-done.4, f32[2,2]{1,0:T(2,128)S(1)} %copy-done.2, s32[8,8]{1,0:T(8,128)S(1)} %copy-done.1, ...), custom_call_target="tpu_custom_call" | custom-call | tf_op jit(solution)/shard_map/own_days/pallas_call | solution.py:530
  2.9 0.0 collective-permute-done
  2.9 0.7 %edges.1 = (f32[32,128]{1,0:T(8,128)S(1)}, f32[32,128]{1,0:T(8,128)S(1)}) custom-call(f32[43,8,128]{2,1,0:T(8,128)S(1)} %get-tuple-element.26.value_ref, f32[6,32,128]{2,1,0:T(8,128)S(1)} %get-tuple-element.27.refs_0_, f32[6,32,128]{2,1,0:T(8,128)S(1)} %get-tuple-element.28.refs_1_, f32[2,3,32,8,128]{4,3,2,1,0:T(8,128)S(1)} %bitcast.13), custom_call_target="tpu_custom_call" | custom-call | tf_op jit(solution)/shard_map/edges/pallas_call | solution.py:543
  3.6 1.6 %collective-permute-start.1 = (f32[32,128]{1,0:T(8,128)S(1)}, f32[32,128]{1,0:T(8,128)S(1)}, u32[]{:S(2)}, u32[]{:S(2)}) collective-permute-start(f32[32,128]{1,0:T(8,128)S(1)} %get-tuple-element.29), channel_id=1, source_target_pairs={{0,1},{1,0},{2,4},{3,5},{4,2},{5,3},{6,7},{7,6},{8,9},{9,8},{10,12... | collective-permute-start | bytes 49160 | tf_op jit(solution)/shard_map/ppermute | solution.py:502
  5.2 0.0 collective-permute-start.2
  5.2 0.7 %copy-done.5 = f32[2,5]{1,0:T(2,128)S(1)} copy-done((f32[2,5]{1,0:T(2,128)S(1)}, f32[2,5]{1,0:T(2,128)}, u32[]{:S(2)}) %copy-start.5) | copy-done | bytes 64
  5.9 1.0 %mix.1 = (f32[6,32,8,128]{3,2,1,0:T(8,128)S(1)}, f32[7,2,8,128]{3,2,1,0:T(8,128)S(1)}, f32[7,2,8,128]{3,2,1,0:T(8,128)S(1)}, bf16[512,256]{1,0:T(8,128)(2,1)S(1)...) custom-call(s32[2]{0:T(128)S(1)} %pad_add_fusion.place_ref, s32[8]{0:T(128)S(1)} %copy-done.3, f32[4]{0:T(128)S(1)} %copy-done.4, ...), custom_call_target="tpu_custom_call" | custom-call | flops 3932160 | bytes 2359296 | tf_op jit(solution)/shard_map/mix/pallas_call | solution.py:553
  6.9 1.4 %collective-permute-done.1.second_ref = f32[32,128]{1,0:T(8,128)S(1)} collective-permute-done((f32[32,128]{1,0:T(8,128)S(1)}, f32[32,128]{1,0:T(8,128)S(1)}, u32[]{:S(2)}, u32[]{:S(2)}) %collective-permute-start.1) | collective-permute-done | bytes 16416 | tf_op jit(solution)/shard_map/ppermute | solution.py:502
  8.3 0.6 %collective-permute-done.2.first_ref = f32[32,128]{1,0:T(8,128)S(1)} collective-permute-done((f32[32,128]{1,0:T(8,128)S(1)}, f32[32,128]{1,0:T(8,128)S(1)}, u32[]{:S(2)}, u32[]{:S(2)}) %collective-permute-start.2) | collective-permute-done | bytes 16416 | tf_op jit(solution)/shard_map/ppermute | solution.py:502
  8.9 1.6 %collective-permute-start.3 = (f32[7,2,8,128]{3,2,1,0:T(8,128)S(1)}, f32[7,2,8,128]{3,2,1,0:T(8,128)S(1)}, u32[]{:S(2)}, u32[]{:S(2)}) collective-permute-start(f32[7,2,8,128]{3,2,1,0:T(8,128)S(1)} %get-tuple-element.34), channel_id=1, source_target_pairs={{0,8},{1,9},{2,10},{3,11},{4,12},{5,13},{6,14},{7,15},{8,0},{9,1},... | collective-permute-start | bytes 172040 | tf_op jit(solution)/shard_map/ppermute | solution.py:502
  10.5 0.0 collective-permute-start.4
  10.5 2.1 %inner_rows.1 = (f32[6,32,8,128]{3,2,1,0:T(8,128)}, f32[6,4,8,128]{3,2,1,0:T(8,128)S(1)}) custom-call(f32[6,8,128]{2,1,0:T(8,128)S(1)} %get-tuple-element.22.level_ref, s32[15,8,128]{2,1,0:T(8,128)S(1)} %get-tuple-element.23.plan_ref, bf16[512,256]{1,0:T(8,128)(2,1)S(1)} %get-tuple-element.24.bands_ref, ...), custom_call_target="tpu_custom_call" | custom-call | flops 100663296 | bytes 1572864 | tf_op jit(solution)/shard_map/inner_rows/pallas_call | solution.py:589
  12.6 0.5 %collective-permute-done.3.first_ref = f32[7,2,8,128]{3,2,1,0:T(8,128)S(1)} collective-permute-done((f32[7,2,8,128]{3,2,1,0:T(8,128)S(1)}, f32[7,2,8,128]{3,2,1,0:T(8,128)S(1)}, u32[]{:S(2)}, u32[]{:S(2)}) %collective-permute-start.3) | collective-permute-done | bytes 57376 | tf_op jit(solution)/shard_map/ppermute | solution.py:502
  13.1 1.6 %collective-permute-done.4.second_ref = f32[7,2,8,128]{3,2,1,0:T(8,128)S(1)} collective-permute-done((f32[7,2,8,128]{3,2,1,0:T(8,128)S(1)}, f32[7,2,8,128]{3,2,1,0:T(8,128)S(1)}, u32[]{:S(2)}, u32[]{:S(2)}) %collective-permute-start.4) | collective-permute-done | bytes 57376 | tf_op jit(solution)/shard_map/ppermute | solution.py:502
  14.7 1.0 %outer_rows.1 = f32[6,32,8,128]{3,2,1,0:T(8,128)} custom-call(f32[6,8,128]{2,1,0:T(8,128)S(1)} %get-tuple-element.22.level_ref, s32[15,8,128]{2,1,0:T(8,128)S(1)} %get-tuple-element.23.plan_ref, bf16[512,256]{1,0:T(8,128)(2,1)S(1)} %get-tuple-element.24.bands_ref, f32[6,4,8,128]{3,2,1,0:T(8,128)S(1)} %get-tuple-element.31.outer_ref, ...), custom_call_target="tpu_custom_call", output_to_operand_aliasing={{}: (6, {})} | custom-call | tf_op jit(solution)/shard_map/outer_rows/pallas_call | solution.py:606
  (5 shorter events, 0.0 us)
Async XLA Ops:
  0.0 2.9 %collective-permute-start = (f32[2,3,8,4096]{3,2,1,0:T(8,128)}, f32[2,3,8,4096]{3,2,1,0:T(8,128)S(1)}, u32[]{:S(2)}, u32[]{:S(2)}) collective-permute-start(f32[2,3,8,4096]{3,2,1,0:T(8,128)} %param.6), channel_id=1, source_target_pairs={{0,1},{1,0},{2,3},{3,2},{4,5},{5,4},{6,7},{7,6},{8,9},{9,8},{10,11... | collective-permute-start | bytes 2359304 | tf_op jit(solution)/shard_map/ppermute | solution.py:520
  0.0 0.7 %copy-start.1 = (s32[8,8]{1,0:T(8,128)S(1)}, s32[8,8]{1,0:T(8,128)}, u32[]{:S(2)}) copy-start(s32[8,8]{1,0:T(8,128)} %nb_ref.3) | copy-start | bytes 772
  0.0 0.7 %copy-start.4 = (f32[4]{0:T(128)S(1)}, f32[4]{0:T(128)}, u32[]{:S(2)}) copy-start(f32[4]{0:T(128)} %taps_ref.3) | copy-start | bytes 52
  0.1 0.7 %copy-start.2 = (f32[2,2]{1,0:T(2,128)S(1)}, f32[2,2]{1,0:T(2,128)}, u32[]{:S(2)}) copy-start(f32[2,2]{1,0:T(2,128)} %factor_ref.3) | copy-start | bytes 52
  0.1 0.7 %copy-start.3 = (s32[8]{0:T(128)S(1)}, s32[8]{0:T(128)}, u32[]{:S(2)}) copy-start(s32[8]{0:T(128)} %mask_ref.3) | copy-start | bytes 100
  0.8 1.1 %copy-start = (f32[2,3,8,4096]{3,2,1,0:T(8,128)S(1)}, f32[2,3,8,4096]{3,2,1,0:T(8,128)}, u32[]{:S(2)}) copy-start(f32[2,3,8,4096]{3,2,1,0:T(8,128)} %param.6) | copy-start | bytes 2359300
  3.6 4.7 %collective-permute-start.1 = (f32[32,128]{1,0:T(8,128)S(1)}, f32[32,128]{1,0:T(8,128)S(1)}, u32[]{:S(2)}, u32[]{:S(2)}) collective-permute-start(f32[32,128]{1,0:T(8,128)S(1)} %get-tuple-element.29), channel_id=1, source_target_pairs={{0,1},{1,0},{2,4},{3,5},{4,2},{5,3},{6,7},{7,6},{8,9},{9,8},{10,12... | collective-permute-start | bytes 49160 | tf_op jit(solution)/shard_map/ppermute | solution.py:502
  5.2 0.7 %copy-start.5 = (f32[2,5]{1,0:T(2,128)S(1)}, f32[2,5]{1,0:T(2,128)}, u32[]{:S(2)}) copy-start(f32[2,5]{1,0:T(2,128)} %space_ref.1) | copy-start | bytes 124
  5.2 3.7 %collective-permute-start.2 = (f32[32,128]{1,0:T(8,128)S(1)}, f32[32,128]{1,0:T(8,128)S(1)}, u32[]{:S(2)}, u32[]{:S(2)}) collective-permute-start(f32[32,128]{1,0:T(8,128)S(1)} %get-tuple-element.30), channel_id=1, source_target_pairs={{0,2},{1,3},{2,0},{3,1},{4,6},{5,7},{6,4},{7,5},{8,10},{9,11},{10,... | collective-permute-start | bytes 49160 | tf_op jit(solution)/shard_map/ppermute | solution.py:502
  8.9 4.2 %collective-permute-start.3 = (f32[7,2,8,128]{3,2,1,0:T(8,128)S(1)}, f32[7,2,8,128]{3,2,1,0:T(8,128)S(1)}, u32[]{:S(2)}, u32[]{:S(2)}) collective-permute-start(f32[7,2,8,128]{3,2,1,0:T(8,128)S(1)} %get-tuple-element.34), channel_id=1, source_target_pairs={{0,8},{1,9},{2,10},{3,11},{4,12},{5,13},{6,14},{7,15},{8,0},{9,1},... | collective-permute-start | bytes 172040 | tf_op jit(solution)/shard_map/ppermute | solution.py:502
  10.5 4.2 %collective-permute-start.4 = (f32[7,2,8,128]{3,2,1,0:T(8,128)S(1)}, f32[7,2,8,128]{3,2,1,0:T(8,128)S(1)}, u32[]{:S(2)}, u32[]{:S(2)}) collective-permute-start(f32[7,2,8,128]{3,2,1,0:T(8,128)S(1)} %get-tuple-element.35), channel_id=1, source_target_pairs={{0,1},{1,0},{2,3},{3,2},{4,5},{5,4},{6,7},{7,6},{8,16},{9,17},{10,... | collective-permute-start | bytes 172040 | tf_op jit(solution)/shard_map/ppermute | solution.py:502

commit v2 on v1

--- a/solution.py
+++ b/solution.py
@@ -170,7 +170,7 @@
 
 
 def own_kernel(
-    pair, place_ref, mask_ref, taps_ref, factor_ref, nb_ref, x_ref, own_ref, *refs
+    pair, place_ref, mask_ref, taps_ref, factor_ref, nb_ref, x_ref, *refs
 ):
     *edge_refs, value_ref = refs
     comps, days, tiles, slots, _ = x_ref.shape
@@ -182,14 +182,6 @@
         for comp in range(comps):
             for t in range(days):
                 edge_ref[comp * days + t] = live * x_ref[comp, t, :, slot, :]
-    def body(tile, _):
-        for comp in range(comps):
-            values = [x_ref[comp, t, tile] for t in range(days)]
-            for t, total in enumerate(same_days(taps, values)):
-                own_ref[comp * days + t, tile] = total
-        return 0
-
-    lax.fori_loop(0, tiles, body, 0, unroll=4)
 
 
 def edge_kernel(pair, value_ref, *refs):
@@ -294,7 +286,7 @@
 
 
 def mix_kernel(
-    pair, place_ref, mask_ref, taps_ref, factor_ref, space_ref, nb_ref, own_ref, *rest
+    pair, place_ref, mask_ref, taps_ref, factor_ref, space_ref, nb_ref, x_ref, *rest
 ):
     *other_refs, mixed_ref, first_ref, second_ref, bands_ref, level_ref, plan_ref = rest
     build_bands(space_ref, bands_ref)
@@ -310,7 +302,7 @@
     def body(tile, _):
         filtered = []
         for comp in range(comps):
-            totals = [own_ref[comp * days + order[t], tile] for t in range(days)]
+            totals = same_days(taps, [x_ref[comp, order[t], tile] for t in range(days)])
             add_later(taps, totals, [other_refs[-1][comp, order[s], tile] for s in range(days)])
             if not pair:
                 add_earlier(taps, totals, [other_refs[0][comp, s, tile] for s in range(days)])
@@ -527,16 +519,16 @@
     others = [in_tiles(x) for x in others]
     field = array(count, tiles, slots, LANES)
 
-    own, *raw, values = pl.pallas_call(
+    x = in_tiles(input_field)
+    *raw, values = pl.pallas_call(
         functools.partial(own_kernel, pair),
-        out_shape=(field,)
-        + (array(count, tiles, LANES),) * 2
+        out_shape=(array(count, tiles, LANES),) * 2
         + (array(VALUES, slots, LANES),),
         in_specs=[SMEM] * 5 + [WHOLE],
-        out_specs=(WHOLE,) * 4,
+        out_specs=(WHOLE,) * 3,
         compiler_params=PARAMS,
         name="own_days",
-    )(place, active_mask, time_taps, coregion_factor, neighbours, in_tiles(input_field))
+    )(place, active_mask, time_taps, coregion_factor, neighbours, x)
 
     sent_count = count + 1
     sent_shape = array(sent_count, PAIR_ROWS, slots, LANES)
@@ -567,7 +559,7 @@
             flops=20 * field.size, bytes_accessed=12 * field.size, transcendentals=0
         ),
         name="mix",
-    )(place, active_mask, time_taps, coregion_factor, space_taps, neighbours, own, *others)
+    )(place, active_mask, time_taps, coregion_factor, space_taps, neighbours, x, *others)
 
     sent = pl.pallas_call(
         corner_kernel,

time: 15.9 us -> 15.7 us (0.987)
  local copies, waits for them, and re-layouts: 2.49 us -> 1.83 us
  waiting for transfers between devices: 4.16 us -> 4.67 us
    unnamed x12 -> x14, local copies, waits for them, and re-layouts: 2.49 us -> 1.83 us
    ppermute x4, waiting for transfers between devices: 4.15 us -> 4.67 us  [swap_both(): results.append(lax.ppermute(x, ('blk', 'day'), pairs))]
where the time goes in v2:
time: 15.7 us; the launch traced here: 15.5 us
  Pallas kernels  5.74 us (37%)
  waiting for transfers between devices  4.67 us (30%)
  starting transfers between devices  3.14 us (20%)
  local copies, waits for them, and re-layouts  1.83 us (12%)
    ppermute x4, waiting for transfers between devices, swap_both(): results.append(lax.ppermute(x, ('blk', 'day'), pairs))  4.67 us
    ppermute x4, starting transfers between devices, swap_both(): results.append(lax.ppermute(x, ('blk', 'day'), pairs))  3.14 us
    pallas_call x1, Pallas kernels, shards(): pl.pallas_call(inner_kernel, out_shape=(field, array(count, 2 * PAIR_ROWS...  2.05 us
    unnamed x14, local copies, waits for them, and re-layouts  1.83 us
    pallas_call x1, Pallas kernels, shards(): pl.pallas_call(functools.partial(mix_kernel, pair), out_shape=(field, sen...  1.17 us
    pallas_call x1, Pallas kernels, shards(): pl.pallas_call(outer_kernel, out_shape=field, in_specs=[WHOLE] * 6 + [IN_...  0.97 us
    pallas_call x1, Pallas kernels, shards(): pl.pallas_call(functools.partial(own_kernel, pair), out_shape=(array(coun...  0.86 us
    pallas_call x1, Pallas kernels, shards(): pl.pallas_call(functools.partial(edge_kernel, pair), out_shape=(array(til...  0.68 us
  transfers between devices with their start and end apart: 5, of which 4 were waited for; matrix products, arithmetic and copies ran while one was open for 0% of the time, Pallas kernels for 26%

profile of v2, /device:TPU:18, one launch (start us, length us, event | category | flops | bytes accessed | tf_op | source)
XLA Modules:
  0.0 15.5 jit_solution(6296125658042494786)
XLA Ops:
  0.0 0.0 collective-permute-start
  0.0 0.1 pad_add_fusion.place_ref
  0.1 0.6 %copy-done.2 = s32[8,8]{1,0:T(8,128)S(1)} copy-done((s32[8,8]{1,0:T(8,128)S(1)}, s32[8,8]{1,0:T(8,128)}, u32[]{:S(2)}) %copy-start.2) | copy-done | bytes 280
  0.7 0.0 copy-done.5
  0.7 0.1 copy-done.3
  0.8 0.0 copy-done.4
  0.8 1.1 %copy-done = f32[2,3,8,4096]{3,2,1,0:T(8,128)S(1)} copy-done((f32[2,3,8,4096]{3,2,1,0:T(8,128)S(1)}, f32[2,3,8,4096]{3,2,1,0:T(8,128)}, u32[]{:S(2)}) %copy-start) | copy-done | bytes 786456
  1.9 0.9 %own_days.1 = (f32[6,32,128]{2,1,0:T(8,128)S(1)}, f32[6,32,128]{2,1,0:T(8,128)S(1)}, f32[43,8,128]{2,1,0:T(8,128)S(1)}) custom-call(s32[2]{0:T(128)S(1)} %pad_add_fusion.place_ref, s32[8]{0:T(128)S(1)} %copy-done.4, f32[4]{0:T(128)S(1)} %copy-done.5, f32[2,2]{1,0:T(2,128)S(1)} %copy-done.3, s32[8,8]{1,0:T(8,128)S(1)} %copy-done.2, ...), custom_call_target="tpu_custom_call" | custom-call | tf_op jit(solution)/shard_map/own_days/pallas_call | solution.py:523
  2.8 0.0 collective-permute-done
  2.8 0.7 %edges.1 = (f32[32,128]{1,0:T(8,128)S(1)}, f32[32,128]{1,0:T(8,128)S(1)}) custom-call(f32[43,8,128]{2,1,0:T(8,128)S(1)} %get-tuple-element.24.value_ref, f32[6,32,128]{2,1,0:T(8,128)S(1)} %get-tuple-element.25.refs_0_, f32[6,32,128]{2,1,0:T(8,128)S(1)} %get-tuple-element.26.refs_1_, f32[2,3,32,8,128]{4,3,2,1,0:T(8,128)S(1)} %bitcast.15), custom_call_target="tpu_custom_call" | custom-call | tf_op jit(solution)/shard_map/edges/pallas_call | solution.py:535
  3.5 0.0 copy-start.6
  3.5 1.6 %collective-permute-start.1 = (f32[32,128]{1,0:T(8,128)S(1)}, f32[32,128]{1,0:T(8,128)S(1)}, u32[]{:S(2)}, u32[]{:S(2)}) collective-permute-start(f32[32,128]{1,0:T(8,128)S(1)} %get-tuple-element.27), channel_id=1, source_target_pairs={{0,1},{1,0},{2,4},{3,5},{4,2},{5,3},{6,7},{7,6},{8,9},{9,8},{10,12... | collective-permute-start | bytes 49160 | tf_op jit(solution)/shard_map/ppermute | solution.py:494
  5.0 0.0 collective-permute-start.2
  5.0 0.0 copy-done.1
  5.0 0.0 copy-done.6
  5.1 1.2 %mix.1 = (f32[6,32,8,128]{3,2,1,0:T(8,128)S(1)}, f32[7,2,8,128]{3,2,1,0:T(8,128)S(1)}, f32[7,2,8,128]{3,2,1,0:T(8,128)S(1)}, bf16[512,256]{1,0:T(8,128)(2,1)S(1)...) custom-call(s32[2]{0:T(128)S(1)} %pad_add_fusion.place_ref, s32[8]{0:T(128)S(1)} %copy-done.4, f32[4]{0:T(128)S(1)} %copy-done.5, ...), custom_call_target="tpu_custom_call" | custom-call | flops 3932160 | bytes 2359296 | tf_op jit(solution)/shard_map/mix/pallas_call | solution.py:545
  6.2 2.0 %collective-permute-done.1.second_ref = f32[32,128]{1,0:T(8,128)S(1)} collective-permute-done((f32[32,128]{1,0:T(8,128)S(1)}, f32[32,128]{1,0:T(8,128)S(1)}, u32[]{:S(2)}, u32[]{:S(2)}) %collective-permute-start.1) | collective-permute-done | bytes 16416 | tf_op jit(solution)/shard_map/ppermute | solution.py:494
  8.2 0.6 %collective-permute-done.2.first_ref = f32[32,128]{1,0:T(8,128)S(1)} collective-permute-done((f32[32,128]{1,0:T(8,128)S(1)}, f32[32,128]{1,0:T(8,128)S(1)}, u32[]{:S(2)}, u32[]{:S(2)}) %collective-permute-start.2) | collective-permute-done | bytes 16416 | tf_op jit(solution)/shard_map/ppermute | solution.py:494
  8.8 1.6 %collective-permute-start.3 = (f32[7,2,8,128]{3,2,1,0:T(8,128)S(1)}, f32[7,2,8,128]{3,2,1,0:T(8,128)S(1)}, u32[]{:S(2)}, u32[]{:S(2)}) collective-permute-start(f32[7,2,8,128]{3,2,1,0:T(8,128)S(1)} %get-tuple-element.32), channel_id=1, source_target_pairs={{0,8},{1,9},{2,10},{3,11},{4,12},{5,13},{6,14},{7,15},{8,0},{9,1},... | collective-permute-start | bytes 172040 | tf_op jit(solution)/shard_map/ppermute | solution.py:494
  10.4 0.0 collective-permute-start.4
  10.4 2.1 %inner_rows.1 = (f32[6,32,8,128]{3,2,1,0:T(8,128)}, f32[6,4,8,128]{3,2,1,0:T(8,128)S(1)}) custom-call(f32[6,8,128]{2,1,0:T(8,128)S(1)} %get-tuple-element.20.level_ref, s32[15,8,128]{2,1,0:T(8,128)S(1)} %get-tuple-element.21.plan_ref, bf16[512,256]{1,0:T(8,128)(2,1)S(1)} %get-tuple-element.22.bands_ref, ...), custom_call_target="tpu_custom_call" | custom-call | flops 100663296 | bytes 1572864 | tf_op jit(solution)/shard_map/inner_rows/pallas_call | solution.py:581
  12.4 0.5 %collective-permute-done.3.first_ref = f32[7,2,8,128]{3,2,1,0:T(8,128)S(1)} collective-permute-done((f32[7,2,8,128]{3,2,1,0:T(8,128)S(1)}, f32[7,2,8,128]{3,2,1,0:T(8,128)S(1)}, u32[]{:S(2)}, u32[]{:S(2)}) %collective-permute-start.3) | collective-permute-done | bytes 57376 | tf_op jit(solution)/shard_map/ppermute | solution.py:494
  13.0 1.6 %collective-permute-done.4.second_ref = f32[7,2,8,128]{3,2,1,0:T(8,128)S(1)} collective-permute-done((f32[7,2,8,128]{3,2,1,0:T(8,128)S(1)}, f32[7,2,8,128]{3,2,1,0:T(8,128)S(1)}, u32[]{:S(2)}, u32[]{:S(2)}) %collective-permute-start.4) | collective-permute-done | bytes 57376 | tf_op jit(solution)/shard_map/ppermute | solution.py:494
  14.5 1.0 %outer_rows.1 = f32[6,32,8,128]{3,2,1,0:T(8,128)} custom-call(f32[6,8,128]{2,1,0:T(8,128)S(1)} %get-tuple-element.20.level_ref, s32[15,8,128]{2,1,0:T(8,128)S(1)} %get-tuple-element.21.plan_ref, bf16[512,256]{1,0:T(8,128)(2,1)S(1)} %get-tuple-element.22.bands_ref, f32[6,4,8,128]{3,2,1,0:T(8,128)S(1)} %get-tuple-element.29.outer_ref, ...), custom_call_target="tpu_custom_call", output_to_operand_aliasing={{}: (6, {})} | custom-call | tf_op jit(solution)/shard_map/outer_rows/pallas_call | solution.py:598
  (7 shorter events, 0.0 us)
Async XLA Ops:
  0.0 2.8 %collective-permute-start = (f32[2,3,8,4096]{3,2,1,0:T(8,128)}, f32[2,3,8,4096]{3,2,1,0:T(8,128)S(1)}, u32[]{:S(2)}, u32[]{:S(2)}) collective-permute-start(f32[2,3,8,4096]{3,2,1,0:T(8,128)} %param.6), channel_id=1, source_target_pairs={{0,1},{1,0},{2,3},{3,2},{4,5},{5,4},{6,7},{7,6},{8,9},{9,8},{10,11... | collective-permute-start | bytes 2359304 | tf_op jit(solution)/shard_map/ppermute | solution.py:512
  0.0 0.7 %copy-start.2 = (s32[8,8]{1,0:T(8,128)S(1)}, s32[8,8]{1,0:T(8,128)}, u32[]{:S(2)}) copy-start(s32[8,8]{1,0:T(8,128)} %nb_ref.3) | copy-start | bytes 772
  0.0 0.7 %copy-start.5 = (f32[4]{0:T(128)S(1)}, f32[4]{0:T(128)}, u32[]{:S(2)}) copy-start(f32[4]{0:T(128)} %taps_ref.3) | copy-start | bytes 52
  0.1 0.7 %copy-start.3 = (f32[2,2]{1,0:T(2,128)S(1)}, f32[2,2]{1,0:T(2,128)}, u32[]{:S(2)}) copy-start(f32[2,2]{1,0:T(2,128)} %factor_ref.3) | copy-start | bytes 52
  0.1 0.7 %copy-start.4 = (s32[8]{0:T(128)S(1)}, s32[8]{0:T(128)}, u32[]{:S(2)}) copy-start(s32[8]{0:T(128)} %mask_ref.3) | copy-start | bytes 100
  0.8 1.1 %copy-start = (f32[2,3,8,4096]{3,2,1,0:T(8,128)S(1)}, f32[2,3,8,4096]{3,2,1,0:T(8,128)}, u32[]{:S(2)}) copy-start(f32[2,3,8,4096]{3,2,1,0:T(8,128)} %param.6) | copy-start | bytes 2359300
  1.9 3.1 %copy-start.1 = (f32[2,3,8,4096]{3,2,1,0:T(8,128)S(1)}, f32[2,3,8,4096]{3,2,1,0:T(8,128)}, u32[]{:S(2)}) copy-start(f32[2,3,8,4096]{3,2,1,0:T(8,128)} %param.6) | copy-start | bytes 2359300
  3.5 1.6 %copy-start.6 = (f32[2,5]{1,0:T(2,128)S(1)}, f32[2,5]{1,0:T(2,128)}, u32[]{:S(2)}) copy-start(f32[2,5]{1,0:T(2,128)} %space_ref.1) | copy-start | bytes 124
  3.5 4.7 %collective-permute-start.1 = (f32[32,128]{1,0:T(8,128)S(1)}, f32[32,128]{1,0:T(8,128)S(1)}, u32[]{:S(2)}, u32[]{:S(2)}) collective-permute-start(f32[32,128]{1,0:T(8,128)S(1)} %get-tuple-element.27), channel_id=1, source_target_pairs={{0,1},{1,0},{2,4},{3,5},{4,2},{5,3},{6,7},{7,6},{8,9},{9,8},{10,12... | collective-permute-start | bytes 49160 | tf_op jit(solution)/shard_map/ppermute | solution.py:494
  5.0 3.7 %collective-permute-start.2 = (f32[32,128]{1,0:T(8,128)S(1)}, f32[32,128]{1,0:T(8,128)S(1)}, u32[]{:S(2)}, u32[]{:S(2)}) collective-permute-start(f32[32,128]{1,0:T(8,128)S(1)} %get-tuple-element.28), channel_id=1, source_target_pairs={{0,2},{1,3},{2,0},{3,1},{4,6},{5,7},{6,4},{7,5},{8,10},{9,11},{10,... | collective-permute-start | bytes 49160 | tf_op jit(solution)/shard_map/ppermute | solution.py:494
  8.8 4.2 %collective-permute-start.3 = (f32[7,2,8,128]{3,2,1,0:T(8,128)S(1)}, f32[7,2,8,128]{3,2,1,0:T(8,128)S(1)}, u32[]{:S(2)}, u32[]{:S(2)}) collective-permute-start(f32[7,2,8,128]{3,2,1,0:T(8,128)S(1)} %get-tuple-element.32), channel_id=1, source_target_pairs={{0,8},{1,9},{2,10},{3,11},{4,12},{5,13},{6,14},{7,15},{8,0},{9,1},... | collective-permute-start | bytes 172040 | tf_op jit(solution)/shard_map/ppermute | solution.py:494
  10.4 4.2 %collective-permute-start.4 = (f32[7,2,8,128]{3,2,1,0:T(8,128)S(1)}, f32[7,2,8,128]{3,2,1,0:T(8,128)S(1)}, u32[]{:S(2)}, u32[]{:S(2)}) collective-permute-start(f32[7,2,8,128]{3,2,1,0:T(8,128)S(1)} %get-tuple-element.33), channel_id=1, source_target_pairs={{0,1},{1,0},{2,3},{3,2},{4,5},{5,4},{6,7},{7,6},{8,16},{9,17},{10,... | collective-permute-start | bytes 172040 | tf_op jit(solution)/shard_map/ppermute | solution.py:494

commit v3 on v1

--- a/solution.py
+++ b/solution.py
@@ -585,7 +585,7 @@
 
     one, two = swap_both(*sent, lambda i: (i // REACH, REACH), blk // REACH)
 
-    together = 2
+    together = 3
     inner, outer = pl.pallas_call(
         inner_kernel,
         out_shape=(field, array(count, 2 * PAIR_ROWS, slots, LANES)),

time: 15.9 us -> 15.9 us (level)
  Pallas kernels: 5.74 us -> 5.49 us
  waiting for transfers between devices: 4.16 us -> 4.41 us
    ppermute x4, waiting for transfers between devices: 4.15 us -> 4.41 us  [swap_both(): results.append(lax.ppermute(x, ('blk', 'day'), pairs))]
    pallas_call x1, Pallas kernels: 2.05 us -> 1.8 us  [shards(): pl.pallas_call(inner_kernel, out_shape=(field, array(count, 2 * PAIR_ROWS...]
  transfers between devices with their start and end apart: 5 -> 5, of which waited for: 4 -> 4; matrix products, arithmetic and copies ran while one was open for 0% -> 0% of each run, Pallas kernels for 26% -> 24%
where the time goes in v3:
time: 15.9 us; the launch traced here: 15.7 us
  Pallas kernels  5.49 us (35%)
  waiting for transfers between devices  4.41 us (28%)
  starting transfers between devices  3.14 us (20%)
  local copies, waits for them, and re-layouts  2.49 us (16%)
    ppermute x4, waiting for transfers between devices, swap_both(): results.append(lax.ppermute(x, ('blk', 'day'), pairs))  4.41 us
    ppermute x4, starting transfers between devices, swap_both(): results.append(lax.ppermute(x, ('blk', 'day'), pairs))  3.14 us
    unnamed x12, local copies, waits for them, and re-layouts  2.49 us
    pallas_call x1, Pallas kernels, shards(): pl.pallas_call(inner_kernel, out_shape=(field, array(count, 2 * PAIR_ROWS...  1.8 us
    pallas_call x1, Pallas kernels, shards(): pl.pallas_call(functools.partial(mix_kernel, pair), out_shape=(field, sen...  1.02 us
    pallas_call x1, Pallas kernels, shards(): pl.pallas_call(functools.partial(own_kernel, pair), out_shape=(field,) +...  1.01 us
    pallas_call x1, Pallas kernels, shards(): pl.pallas_call(outer_kernel, out_shape=field, in_specs=[WHOLE] * 6 + [IN_...  0.97 us
    pallas_call x1, Pallas kernels, shards(): pl.pallas_call(functools.partial(edge_kernel, pair), out_shape=(array(til...  0.69 us
  transfers between devices with their start and end apart: 5, of which 4 were waited for; matrix products, arithmetic and copies ran while one was open for 0% of the time, Pallas kernels for 24%

profile of v3, /device:TPU:18, one launch (start us, length us, event | category | flops | bytes accessed | tf_op | source)
XLA Modules:
  0.0 15.7 jit_solution(13302127548391984591)
XLA Ops:
  0.0 0.0 collective-permute-start
  0.0 0.0 copy-start.1
  0.0 0.0 copy-start.4
  0.0 0.1 pad_add_fusion.place_ref
  0.1 0.6 %copy-done.1 = s32[8,8]{1,0:T(8,128)S(1)} copy-done((s32[8,8]{1,0:T(8,128)S(1)}, s32[8,8]{1,0:T(8,128)}, u32[]{:S(2)}) %copy-start.1) | copy-done | bytes 280
  0.7 0.0 copy-done.4
  0.7 0.1 copy-done.2
  0.8 0.0 copy-done.3
  0.8 1.1 %copy-done = f32[2,3,8,4096]{3,2,1,0:T(8,128)S(1)} copy-done((f32[2,3,8,4096]{3,2,1,0:T(8,128)S(1)}, f32[2,3,8,4096]{3,2,1,0:T(8,128)}, u32[]{:S(2)}) %copy-start) | copy-done | bytes 786456
  1.9 1.0 %own_days.1 = (f32[6,32,8,128]{3,2,1,0:T(8,128)S(1)}, f32[6,32,128]{2,1,0:T(8,128)S(1)}, f32[6,32,128]{2,1,0:T(8,128)S(1)}, f32[43,8,128]{2,1,0:T(8,128)S(1)}) custom-call(s32[2]{0:T(128)S(1)} %pad_add_fusion.place_ref, s32[8]{0:T(128)S(1)} %copy-done.3, f32[4]{0:T(128)S(1)} %copy-done.4, f32[2,2]{1,0:T(2,128)S(1)} %copy-done.2, s32[8,8]{1,0:T(8,128)S(1)} %copy-done.1, ...), custom_call_target="tpu_custom_call" | custom-call | tf_op jit(solution)/shard_map/own_days/pallas_call | solution.py:530
  2.9 0.0 collective-permute-done
  2.9 0.7 %edges.1 = (f32[32,128]{1,0:T(8,128)S(1)}, f32[32,128]{1,0:T(8,128)S(1)}) custom-call(f32[43,8,128]{2,1,0:T(8,128)S(1)} %get-tuple-element.26.value_ref, f32[6,32,128]{2,1,0:T(8,128)S(1)} %get-tuple-element.27.refs_0_, f32[6,32,128]{2,1,0:T(8,128)S(1)} %get-tuple-element.28.refs_1_, f32[2,3,32,8,128]{4,3,2,1,0:T(8,128)S(1)} %bitcast.13), custom_call_target="tpu_custom_call" | custom-call | tf_op jit(solution)/shard_map/edges/pallas_call | solution.py:543
  3.6 1.6 %collective-permute-start.1 = (f32[32,128]{1,0:T(8,128)S(1)}, f32[32,128]{1,0:T(8,128)S(1)}, u32[]{:S(2)}, u32[]{:S(2)}) collective-permute-start(f32[32,128]{1,0:T(8,128)S(1)} %get-tuple-element.29), channel_id=1, source_target_pairs={{0,1},{1,0},{2,4},{3,5},{4,2},{5,3},{6,7},{7,6},{8,9},{9,8},{10,12... | collective-permute-start | bytes 49160 | tf_op jit(solution)/shard_map/ppermute | solution.py:502
  5.2 0.0 collective-permute-start.2
  5.2 0.7 %copy-done.5 = f32[2,5]{1,0:T(2,128)S(1)} copy-done((f32[2,5]{1,0:T(2,128)S(1)}, f32[2,5]{1,0:T(2,128)}, u32[]{:S(2)}) %copy-start.5) | copy-done | bytes 64
  5.9 1.0 %mix.1 = (f32[6,32,8,128]{3,2,1,0:T(8,128)S(1)}, f32[7,2,8,128]{3,2,1,0:T(8,128)S(1)}, f32[7,2,8,128]{3,2,1,0:T(8,128)S(1)}, bf16[512,256]{1,0:T(8,128)(2,1)S(1)...) custom-call(s32[2]{0:T(128)S(1)} %pad_add_fusion.place_ref, s32[8]{0:T(128)S(1)} %copy-done.3, f32[4]{0:T(128)S(1)} %copy-done.4, ...), custom_call_target="tpu_custom_call" | custom-call | flops 3932160 | bytes 2359296 | tf_op jit(solution)/shard_map/mix/pallas_call | solution.py:553
  6.9 1.4 %collective-permute-done.1.second_ref = f32[32,128]{1,0:T(8,128)S(1)} collective-permute-done((f32[32,128]{1,0:T(8,128)S(1)}, f32[32,128]{1,0:T(8,128)S(1)}, u32[]{:S(2)}, u32[]{:S(2)}) %collective-permute-start.1) | collective-permute-done | bytes 16416 | tf_op jit(solution)/shard_map/ppermute | solution.py:502
  8.3 0.6 %collective-permute-done.2.first_ref = f32[32,128]{1,0:T(8,128)S(1)} collective-permute-done((f32[32,128]{1,0:T(8,128)S(1)}, f32[32,128]{1,0:T(8,128)S(1)}, u32[]{:S(2)}, u32[]{:S(2)}) %collective-permute-start.2) | collective-permute-done | bytes 16416 | tf_op jit(solution)/shard_map/ppermute | solution.py:502
  8.9 1.6 %collective-permute-start.3 = (f32[7,2,8,128]{3,2,1,0:T(8,128)S(1)}, f32[7,2,8,128]{3,2,1,0:T(8,128)S(1)}, u32[]{:S(2)}, u32[]{:S(2)}) collective-permute-start(f32[7,2,8,128]{3,2,1,0:T(8,128)S(1)} %get-tuple-element.34), channel_id=1, source_target_pairs={{0,8},{1,9},{2,10},{3,11},{4,12},{5,13},{6,14},{7,15},{8,0},{9,1},... | collective-permute-start | bytes 172040 | tf_op jit(solution)/shard_map/ppermute | solution.py:502
  10.5 0.0 collective-permute-start.4
  10.5 1.8 %inner_rows.1 = (f32[6,32,8,128]{3,2,1,0:T(8,128)}, f32[6,4,8,128]{3,2,1,0:T(8,128)S(1)}) custom-call(f32[6,8,128]{2,1,0:T(8,128)S(1)} %get-tuple-element.22.level_ref, s32[15,8,128]{2,1,0:T(8,128)S(1)} %get-tuple-element.23.plan_ref, bf16[512,256]{1,0:T(8,128)(2,1)S(1)} %get-tuple-element.24.bands_ref, ...), custom_call_target="tpu_custom_call" | custom-call | flops 100663296 | bytes 1572864 | tf_op jit(solution)/shard_map/inner_rows/pallas_call | solution.py:589
  12.3 0.8 %collective-permute-done.3.first_ref = f32[7,2,8,128]{3,2,1,0:T(8,128)S(1)} collective-permute-done((f32[7,2,8,128]{3,2,1,0:T(8,128)S(1)}, f32[7,2,8,128]{3,2,1,0:T(8,128)S(1)}, u32[]{:S(2)}, u32[]{:S(2)}) %collective-permute-start.3) | collective-permute-done | bytes 57376 | tf_op jit(solution)/shard_map/ppermute | solution.py:502
  13.1 1.6 %collective-permute-done.4.second_ref = f32[7,2,8,128]{3,2,1,0:T(8,128)S(1)} collective-permute-done((f32[7,2,8,128]{3,2,1,0:T(8,128)S(1)}, f32[7,2,8,128]{3,2,1,0:T(8,128)S(1)}, u32[]{:S(2)}, u32[]{:S(2)}) %collective-permute-start.4) | collective-permute-done | bytes 57376 | tf_op jit(solution)/shard_map/ppermute | solution.py:502
  14.7 1.0 %outer_rows.1 = f32[6,32,8,128]{3,2,1,0:T(8,128)} custom-call(f32[6,8,128]{2,1,0:T(8,128)S(1)} %get-tuple-element.22.level_ref, s32[15,8,128]{2,1,0:T(8,128)S(1)} %get-tuple-element.23.plan_ref, bf16[512,256]{1,0:T(8,128)(2,1)S(1)} %get-tuple-element.24.bands_ref, f32[6,4,8,128]{3,2,1,0:T(8,128)S(1)} %get-tuple-element.31.outer_ref, ...), custom_call_target="tpu_custom_call", output_to_operand_aliasing={{}: (6, {})} | custom-call | tf_op jit(solution)/shard_map/outer_rows/pallas_call | solution.py:606
  (5 shorter events, 0.0 us)
Async XLA Ops:
  0.0 2.9 %collective-permute-start = (f32[2,3,8,4096]{3,2,1,0:T(8,128)}, f32[2,3,8,4096]{3,2,1,0:T(8,128)S(1)}, u32[]{:S(2)}, u32[]{:S(2)}) collective-permute-start(f32[2,3,8,4096]{3,2,1,0:T(8,128)} %param.6), channel_id=1, source_target_pairs={{0,1},{1,0},{2,3},{3,2},{4,5},{5,4},{6,7},{7,6},{8,9},{9,8},{10,11... | collective-permute-start | bytes 2359304 | tf_op jit(solution)/shard_map/ppermute | solution.py:520
  0.0 0.7 %copy-start.1 = (s32[8,8]{1,0:T(8,128)S(1)}, s32[8,8]{1,0:T(8,128)}, u32[]{:S(2)}) copy-start(s32[8,8]{1,0:T(8,128)} %nb_ref.3) | copy-start | bytes 772
  0.0 0.7 %copy-start.4 = (f32[4]{0:T(128)S(1)}, f32[4]{0:T(128)}, u32[]{:S(2)}) copy-start(f32[4]{0:T(128)} %taps_ref.3) | copy-start | bytes 52
  0.1 0.7 %copy-start.2 = (f32[2,2]{1,0:T(2,128)S(1)}, f32[2,2]{1,0:T(2,128)}, u32[]{:S(2)}) copy-start(f32[2,2]{1,0:T(2,128)} %factor_ref.3) | copy-start | bytes 52
  0.1 0.7 %copy-start.3 = (s32[8]{0:T(128)S(1)}, s32[8]{0:T(128)}, u32[]{:S(2)}) copy-start(s32[8]{0:T(128)} %mask_ref.3) | copy-start | bytes 100
  0.8 1.1 %copy-start = (f32[2,3,8,4096]{3,2,1,0:T(8,128)S(1)}, f32[2,3,8,4096]{3,2,1,0:T(8,128)}, u32[]{:S(2)}) copy-start(f32[2,3,8,4096]{3,2,1,0:T(8,128)} %param.6) | copy-start | bytes 2359300
  3.6 4.7 %collective-permute-start.1 = (f32[32,128]{1,0:T(8,128)S(1)}, f32[32,128]{1,0:T(8,128)S(1)}, u32[]{:S(2)}, u32[]{:S(2)}) collective-permute-start(f32[32,128]{1,0:T(8,128)S(1)} %get-tuple-element.29), channel_id=1, source_target_pairs={{0,1},{1,0},{2,4},{3,5},{4,2},{5,3},{6,7},{7,6},{8,9},{9,8},{10,12... | collective-permute-start | bytes 49160 | tf_op jit(solution)/shard_map/ppermute | solution.py:502
  5.2 0.7 %copy-start.5 = (f32[2,5]{1,0:T(2,128)S(1)}, f32[2,5]{1,0:T(2,128)}, u32[]{:S(2)}) copy-start(f32[2,5]{1,0:T(2,128)} %space_ref.1) | copy-start | bytes 124
  5.2 3.7 %collective-permute-start.2 = (f32[32,128]{1,0:T(8,128)S(1)}, f32[32,128]{1,0:T(8,128)S(1)}, u32[]{:S(2)}, u32[]{:S(2)}) collective-permute-start(f32[32,128]{1,0:T(8,128)S(1)} %get-tuple-element.30), channel_id=1, source_target_pairs={{0,2},{1,3},{2,0},{3,1},{4,6},{5,7},{6,4},{7,5},{8,10},{9,11},{10,... | collective-permute-start | bytes 49160 | tf_op jit(solution)/shard_map/ppermute | solution.py:502
  8.9 4.2 %collective-permute-start.3 = (f32[7,2,8,128]{3,2,1,0:T(8,128)S(1)}, f32[7,2,8,128]{3,2,1,0:T(8,128)S(1)}, u32[]{:S(2)}, u32[]{:S(2)}) collective-permute-start(f32[7,2,8,128]{3,2,1,0:T(8,128)S(1)} %get-tuple-element.34), channel_id=1, source_target_pairs={{0,8},{1,9},{2,10},{3,11},{4,12},{5,13},{6,14},{7,15},{8,0},{9,1},... | collective-permute-start | bytes 172040 | tf_op jit(solution)/shard_map/ppermute | solution.py:502
  10.5 4.2 %collective-permute-start.4 = (f32[7,2,8,128]{3,2,1,0:T(8,128)S(1)}, f32[7,2,8,128]{3,2,1,0:T(8,128)S(1)}, u32[]{:S(2)}, u32[]{:S(2)}) collective-permute-start(f32[7,2,8,128]{3,2,1,0:T(8,128)S(1)} %get-tuple-element.35), channel_id=1, source_target_pairs={{0,1},{1,0},{2,3},{3,2},{4,5},{5,4},{6,7},{7,6},{8,16},{9,17},{10,... | collective-permute-start | bytes 172040 | tf_op jit(solution)/shard_map/ppermute | solution.py:502
